TPU v7x, 32 devices: a whole 2x2x4 slice. The times are simulated.
32 devices in a mesh: seq: 16 (over z, x, core), store: 2 (over y).
Axes of the slice: x: 2, y: 2, z: 4, core: 2. Of those that a mesh axis runs over, the one named last changes fastest.
Arguments:
- queries: bfloat16 [2, 2048, 4096], P('store', 'seq'), may hold values from -12 to 12
- keys: bfloat16 [2, 2048, 512], P('store', 'seq'), may hold values from -6 to 6
- values: bfloat16 [2, 2048, 512], P('store', 'seq'), may hold values from -6 to 6
- segment_ids: int32 [2, 2048], P('store', 'seq'), may hold values from 0 to 3, never falling along the last dimension, each value on 1 to 1024 neighbouring positions
- route_ids: int32 [2, 2048], P('store', 'seq'), may hold values from 0 to 511, as said below
- adapter_down: bfloat16 [4096, 32768], P(None, ('seq', 'store')), may hold values from -0.09375 to 0.09375
- adapter_up: bfloat16 [32768, 4096], P(('seq', 'store')), may hold values from -0.75 to 0.75
Outputs:
- mixed: bfloat16 [2, 2048, 4096], P('store', 'seq')
Inputs may be any that keep to these rules, and one draw needn't show every extreme that they name: `route_ids`: among the 128 tokens of one device (positions j * 128 to j * 128 + 127 of one sequence), at most 8 name adapters of any one owner, the owner of adapter e being the device of flat index e // 16 over seq then store; in every draw some owner gets exactly 8 tokens from every device.
All inputs are finite; a program needn't handle non-finite values.
Results may differ from a plain program's by a relative error of at most 0.006.
Values may be sent and summed in bfloat16 or wider, within the bound.
A program may use at most 128 MiB of HBM per device.

v0:
```python
import jax
import jax.numpy as jnp
from jax import lax
from jax.sharding import PartitionSpec as P

HEAD_DIM = 128
HEADS = 32
KV_HEADS = 4
RANK = 64
EXP_DEV = 16


def attend(queries, key_rows, value_rows, segments):
    length = queries.shape[0]
    block = min(512, length)
    scale = queries.shape[2] ** (-0.5)
    key_pos = jnp.arange(length, dtype=jnp.int32)

    def one_block(index):
        start = index * block
        q_block = lax.dynamic_slice_in_dim(queries, start, block, 0)
        seg_block = lax.dynamic_slice_in_dim(segments, start, block, 0)
        scores = (
            jnp.einsum("qhd,nd->hqn", q_block, key_rows, preferred_element_type=jnp.float32) * scale
        )
        q_pos = start + jnp.arange(block, dtype=jnp.int32)
        allowed = (key_pos[None, :] <= q_pos[:, None]) & (segments[None, :] == seg_block[:, None])
        scores = jnp.where(allowed[None], scores, jnp.float32(-1e30))
        top = jnp.max(scores, axis=-1, keepdims=True)
        expo = jnp.exp(scores - top)
        total = jnp.sum(expo, axis=-1)
        summed = jnp.einsum(
            "hqn,nd->qhd", expo.astype(jnp.bfloat16), value_rows, preferred_element_type=jnp.float32
        )
        out = summed / jnp.transpose(total)[:, :, None]
        return out.astype(jnp.bfloat16).reshape(block, -1)

    blocks = lax.map(one_block, jnp.arange(length // block, dtype=jnp.int32))
    return blocks.reshape(length, -1)


def local(queries, keys, values, segment_ids, route_ids, adapter_down, adapter_up):
    n_seq = lax.axis_size("seq")
    n_store = lax.axis_size("store")
    tok_rows = queries.shape[1]
    width = queries.shape[2]
    length = tok_rows * n_seq
    heads_here = HEADS // n_seq
    q_send = queries.reshape(tok_rows, n_seq, heads_here * HEAD_DIM)
    paired = jnp.concatenate(
        [keys.reshape(tok_rows, KV_HEADS, HEAD_DIM), values.reshape(tok_rows, KV_HEADS, HEAD_DIM)],
        axis=2,
    )
    kv_send = jnp.repeat(paired, n_seq // KV_HEADS, axis=1)
    q_all, kv_all = (
        lax.all_to_all(q_send, "seq", split_axis=1, concat_axis=0, tiled=True),
        lax.all_to_all(kv_send, "seq", split_axis=1, concat_axis=0, tiled=True),
    )
    segments = lax.all_gather(segment_ids, "seq", axis=1, tiled=True)[0]
    context = attend(
        q_all.reshape(length, heads_here, HEAD_DIM),
        kv_all[:, 0, :HEAD_DIM],
        kv_all[:, 0, HEAD_DIM:],
        segments,
    )
    returned_ctx = lax.all_to_all(
        context.reshape(length, 1, heads_here * HEAD_DIM),
        "seq",
        split_axis=0,
        concat_axis=1,
        tiled=True,
    )
    tok_ctx = returned_ctx.reshape(tok_rows, width)
    devices = n_seq * n_store
    capacity = max(2, 2 * tok_rows // devices)
    chosen = route_ids[0]
    owners = chosen // EXP_DEV
    one_hot = (owners[:, None] == jnp.arange(devices, dtype=jnp.int32)[None, :]).astype(jnp.int32)
    slot_of = jnp.sum(jnp.cumsum(one_hot, axis=0) * one_hot, axis=1) - 1
    placed = owners * capacity + slot_of
    send_rows = jnp.zeros((devices * capacity, width), jnp.bfloat16).at[placed].set(tok_ctx)
    send_tags = (
        jnp.full((devices * capacity,), -1.0, jnp.float32)
        .at[placed]
        .set((chosen % EXP_DEV).astype(jnp.float32))
        .astype(jnp.bfloat16)
    )
    got_rows = lax.all_to_all(
        send_rows.reshape(devices, capacity, width),
        ("seq", "store"),
        split_axis=0,
        concat_axis=0,
        tiled=True,
    )
    flat_rows = got_rows.reshape(-1, width)
    low = jnp.dot(flat_rows, adapter_down, preferred_element_type=jnp.float32)
    lane_owner = (jnp.arange(low.shape[1], dtype=jnp.int32) // RANK).astype(jnp.float32)
    keep_mask = (
        lax.all_to_all(
            send_tags.reshape(devices, capacity),
            ("seq", "store"),
            split_axis=0,
            concat_axis=0,
            tiled=True,
        )
        .reshape(-1, 1)
        .astype(jnp.float32)
        == lane_owner[None, :]
    )
    low = jnp.where(keep_mask, low, 0.0).astype(jnp.bfloat16)
    delta = jnp.dot(low, adapter_up, preferred_element_type=jnp.float32).astype(jnp.bfloat16)
    answer = lax.all_to_all(
        delta.reshape(got_rows.shape), ("seq", "store"), split_axis=0, concat_axis=0, tiled=True
    )
    delta_rows = answer.reshape(devices * capacity, width)[placed]
    mixed = (tok_ctx.astype(jnp.float32) + delta_rows.astype(jnp.float32)).astype(jnp.bfloat16)
    return mixed[None]


def solution(mesh):
    return jax.shard_map(
        local,
        mesh=mesh,
        in_specs=(
            P("store", "seq", None),
            P("store", "seq", None),
            P("store", "seq", None),
            P("store", "seq"),
            P("store", "seq"),
            P(None, ("seq", "store")),
            P(("seq", "store"), None),
        ),
        out_specs=P("store", "seq", None),
        check_vma=False,
    )
```

profile of v0, /device:TPU:27, one launch (start us, length us, event | category | flops | bytes accessed | tf_op | source)
XLA Modules:
  0.0 288.1 jit_solution(12648538847451133747)
XLA Ops:
  0.0 2.3 copy.30
  2.3 6.3 %all-to-all-start = ((bf16[128,16,256]{0,2,1:T(8,128)(2,1)}), bf16[128,16,256]{0,2,1:T(8,128)(2,1)S(1)}, u32[]{:S(2)}, u32[]{:S(2)}) async-start(bf16[128,16,256]{0,2,1:T(8,128)(2,1)} %bitcast.1), calls=%async_computation | async-start | bytes 2097152 | tf_op jit(solution)/shard_map/all_to_all | solution.py:56
  8.6 0.9 reshape.261
  9.5 0.9 reshape.260
  10.5 0.1 pad_maximum_fusion
  10.7 21.9 %all-to-all-done = bf16[128,16,256]{0,2,1:T(8,128)(2,1)S(1)} async-done(((bf16[128,16,256]{0,2,1:T(8,128)(2,1)}), bf16[128,16,256]{0,2,1:T(8,128)(2,1)S(1)}, u32[]{:S(2)}, u32[]{:S(2)}) %all-to-all-start) | async-done | bytes 1048608 | tf_op jit(solution)/shard_map/all_to_all | solution.py:56
  32.6 1.1 broadcast_in_dim.46
  33.7 5.9 %all-to-all-start.1 = ((bf16[128,16,256]{2,0,1:T(8,128)(2,1)}), bf16[128,16,256]{2,0,1:T(8,128)(2,1)S(1)}, u32[]{:S(2)}, u32[]{:S(2)}) async-start(bf16[128,16,256]{2,0,1:T(8,128)(2,1)} %bitcast.4), calls=%async_computation.1 | async-start | bytes 2097152 | tf_op jit(solution)/shard_map/all_to_all | solution.py:57
  39.6 33.3 %all_gather.3 = s32[1,2048]{1,0:T(1,128)S(1)} all-gather(s32[1,128]{1,0:T(1,128)S(1)} %copy-done), channel_id=1, replica_groups=mesh['seq'=16,'store'=2] {'seq'}, dimensions={1}, use_global_device_ids=true | all-gather | bytes 8704 | tf_op jit(solution)/shard_map/all_gather | solution.py:59
  72.9 0.7 copy.31
  73.6 1.3 reshape.259
  75.0 0.2 copy.34
  75.2 46.3 %while.11 = (s32[]{:T(128)}, bf16[4,512,256]{2,1,0:T(8,128)(2,1)}, s32[4]{0:T(128)S(1)}, s32[1,2048]{1,0:T(1,128)S(1)}, s32[2048]{0:T(1024)S(1)}, /*index=5*/bf1...) while((s32[]{:T(128)}, bf16[4,512,256]{2,1,0:T(8,128)(2,1)}, ...), condition=%wide.region_3.4_spmd.clone, body=%wide.region_0.3_spmd.clone.sunk | while | flops 1100216832 | bytes 32020680 | solution.py:38
  75.2 0.7 dynamic_slice.21
  76.7 1.0 fusion.61
  77.7 3.2 %bitcast_reduce_fusion.2 = (f32[2,512]{1,0:T(2,128)S(1)}, f32[512,2,2048]{2,0,1:T(8,128)S(1)}) fusion(pred[512,2048]{1,0:T(8,128)(4,1)S(1)} %fusion.61, bf16[2048,128]{1,0:T(8,128)(2,1)S(1)} %get-tuple-element.208, bf16[2048,2,128]{0,2,1:T(8,128)(2,1)} %get-tuple-element.207, s32[]{:T(128)S(6)} %select_n.110), kind=kOutput, calls=%fused_computation.5.clone.1 | convolution fusion | flops 543161344 | bytes 10227716 | tf_op jit(solution)/shard_map/while/body/eval_jaxpr/qhd,nd->hqn/dot_general | solution.py:24
  80.9 2.6 fusion.62
  83.5 2.5 fusion.63
  85.9 0.1 copy.47
  86.1 0.7 constant_dynamic-update-slice_fusion.2
  86.8 0.7 dynamic_slice.21
  88.2 1.0 fusion.61
  89.3 3.2 %bitcast_reduce_fusion.2 = (f32[2,512]{1,0:T(2,128)S(1)}, f32[512,2,2048]{2,0,1:T(8,128)S(1)}) fusion(pred[512,2048]{1,0:T(8,128)(4,1)S(1)} %fusion.61, bf16[2048,128]{1,0:T(8,128)(2,1)S(1)} %get-tuple-element.208, bf16[2048,2,128]{0,2,1:T(8,128)(2,1)} %get-tuple-element.207, s32[]{:T(128)S(6)} %select_n.110), kind=kOutput, calls=%fused_computation.5.clone.1 | convolution fusion | flops 543161344 | bytes 10227716 | tf_op jit(solution)/shard_map/while/body/eval_jaxpr/qhd,nd->hqn/dot_general | solution.py:24
  92.5 2.6 fusion.62
  95.1 2.5 fusion.63
  97.5 0.1 copy.47
  97.7 0.7 constant_dynamic-update-slice_fusion.2
  98.4 0.7 dynamic_slice.21
  99.8 1.0 fusion.61
  100.9 3.2 %bitcast_reduce_fusion.2 = (f32[2,512]{1,0:T(2,128)S(1)}, f32[512,2,2048]{2,0,1:T(8,128)S(1)}) fusion(pred[512,2048]{1,0:T(8,128)(4,1)S(1)} %fusion.61, bf16[2048,128]{1,0:T(8,128)(2,1)S(1)} %get-tuple-element.208, bf16[2048,2,128]{0,2,1:T(8,128)(2,1)} %get-tuple-element.207, s32[]{:T(128)S(6)} %select_n.110), kind=kOutput, calls=%fused_computation.5.clone.1 | convolution fusion | flops 543161344 | bytes 10227716 | tf_op jit(solution)/shard_map/while/body/eval_jaxpr/qhd,nd->hqn/dot_general | solution.py:24
  104.1 2.6 fusion.62
  106.6 2.5 fusion.63
  109.1 0.1 copy.47
  109.2 0.7 constant_dynamic-update-slice_fusion.2
  110.0 0.7 dynamic_slice.21
  111.4 1.0 fusion.61
  112.4 3.2 %bitcast_reduce_fusion.2 = (f32[2,512]{1,0:T(2,128)S(1)}, f32[512,2,2048]{2,0,1:T(8,128)S(1)}) fusion(pred[512,2048]{1,0:T(8,128)(4,1)S(1)} %fusion.61, bf16[2048,128]{1,0:T(8,128)(2,1)S(1)} %get-tuple-element.208, bf16[2048,2,128]{0,2,1:T(8,128)(2,1)} %get-tuple-element.207, s32[]{:T(128)S(6)} %select_n.110), kind=kOutput, calls=%fused_computation.5.clone.1 | convolution fusion | flops 543161344 | bytes 10227716 | tf_op jit(solution)/shard_map/while/body/eval_jaxpr/qhd,nd->hqn/dot_general | solution.py:24
  115.7 2.6 fusion.62
  118.2 2.5 fusion.63
  120.8 0.7 constant_dynamic-update-slice_fusion.2
  121.5 0.6 broadcast.244
  122.1 2.7 reduce.4
  124.9 1.1 reshape.308
  126.0 5.9 %all-to-all-start.2 = ((bf16[16,2,16384]{2,1,0:T(2,128)(2,1)}), bf16[16,2,16384]{2,1,0:T(2,128)(2,1)S(1)}, u32[]{:S(2)}, u32[]{:S(2)}) async-start(bf16[16,2,16384]{2,1,0:T(2,128)(2,1)} %reshape.308), calls=%async_computation.2 | async-start | bytes 2097152 | tf_op jit(solution)/shard_map/all_to_all | solution.py:66
  132.0 0.2 reduce_window_sum.11
  132.1 0.2 select_reduce_fusion
  132.3 1.0 scatter_custom_fusion
  133.3 0.7 all_to_all.61
  134.0 21.8 %all-to-all-done.2 = bf16[16,2,16384]{2,1,0:T(2,128)(2,1)S(1)} async-done(((bf16[16,2,16384]{2,1,0:T(2,128)(2,1)}), bf16[16,2,16384]{2,1,0:T(2,128)(2,1)S(1)}, u32[]{:S(2)}, u32[]{:S(2)}) %all-to-all-start.2) | async-done | bytes 1048608 | tf_op jit(solution)/shard_map/all_to_all | solution.py:66
  155.8 5.7 %all-to-all-start.3 = ((bf16[32,1,8]{2,1,0:T(2,128)(2,1)}), bf16[32,1,8]{2,1,0:T(2,128)(2,1)S(1)}, u32[]{:S(2)}, u32[]{:S(2)}) async-start(bf16[32,1,8]{2,1,0:T(2,128)(2,1)} %all_to_all.61), calls=%async_computation.3 | async-start | bytes 32768 | tf_op jit(solution)/shard_map/all_to_all | solution.py:99
  161.5 1.1 reshape.309
  162.6 0.2 copy.44
  162.8 0.7 copy.39
  163.4 0.5 copy.40
  164.0 3.7 %scatter_custom_fusion.1 = bf16[256,4096]{1,0:T(8,128)(2,1)} fusion(s32[128]{0:T(128)S(1)} %fusion.48, bf16[128,4096]{1,0:T(8,128)(2,1)S(1)} %copy.40, bf16[]{:T(256)} %constant.71.clone.1), kind=kCustom, calls=%fused_computation.34 | custom fusion | bytes 2097154 | tf_op jit(solution)/shard_map/scatter | solution.py:81
  167.6 5.8 %all-to-all-start.4 = ((bf16[32,8,4096]{2,1,0:T(8,128)(2,1)}), bf16[32,8,4096]{2,1,0:T(8,128)(2,1)S(1)}, u32[]{:S(2)}, u32[]{:S(2)}) async-start(bf16[32,8,4096]{2,1,0:T(8,128)(2,1)} %bitcast.19), calls=%async_computation.4 | async-start | bytes 4194304 | tf_op jit(solution)/shard_map/all_to_all | solution.py:88
  173.6 46.4 %all-to-all-done.4 = bf16[32,8,4096]{2,1,0:T(8,128)(2,1)S(1)} async-done(((bf16[32,8,4096]{2,1,0:T(8,128)(2,1)}), bf16[32,8,4096]{2,1,0:T(8,128)(2,1)S(1)}, u32[]{:S(2)}, u32[]{:S(2)}) %all-to-all-start.4) | async-done | bytes 2097184 | tf_op jit(solution)/shard_map/all_to_all | solution.py:88
  220.1 11.6 %fusion.25 = bf16[32,8,4096]{2,1,0:T(8,128)(2,1)} fusion(bf16[1024,4096]{1,0:T(8,128)(2,1)} %param.15, bf16[4096,1024]{1,0:T(8,128)(2,1)} %param.14, bf16[32,8,4096]{2,1,0:T(8,128)(2,1)S(1)} %all-to-all-done.4, f32[1024]{0:T(1024)S(1)} %fusion.43, f32[256]{0:T(256)S(1)} %reshape.269), kind=kOutput, calls=%fused_computation.27 | convolution fusion | flops 4296802304 | bytes 20976640 | tf_op jit(solution)/shard_map/dot_general | solution.py:111
  231.7 5.8 %all-to-all-start.5 = ((bf16[32,8,4096]{2,1,0:T(8,128)(2,1)}), bf16[32,8,4096]{2,1,0:T(8,128)(2,1)S(1)}, u32[]{:S(2)}, u32[]{:S(2)}) async-start(bf16[32,8,4096]{2,1,0:T(8,128)(2,1)} %fusion.25), calls=%async_computation.5 | async-start | bytes 4194304 | tf_op jit(solution)/shard_map/all_to_all | solution.py:112
  237.5 1.9 copy.37
  239.4 2.7 reshape.268
  242.2 41.9 %all-to-all-done.5 = bf16[32,8,4096]{2,1,0:T(8,128)(2,1)S(1)} async-done(((bf16[32,8,4096]{2,1,0:T(8,128)(2,1)}), bf16[32,8,4096]{2,1,0:T(8,128)(2,1)S(1)}, u32[]{:S(2)}, u32[]{:S(2)}) %all-to-all-start.5) | async-done | bytes 2097184 | tf_op jit(solution)/shard_map/all_to_all | solution.py:112
  284.1 1.2 gather_fusion
  285.3 2.8 fusion.26
  (27 shorter events, 0.8 us)
Async XLA Ops:
  0.0 39.6 %copy-start = (s32[1,128]{1,0:T(1,128)S(1)}, s32[1,128]{1,0:T(1,128)}, u32[]{:S(2)}) copy-start(s32[1,128]{1,0:T(1,128)} %param.12) | copy-start | bytes 1540
  2.3 30.3 %all-to-all-start = ((bf16[128,16,256]{0,2,1:T(8,128)(2,1)}), bf16[128,16,256]{0,2,1:T(8,128)(2,1)S(1)}, u32[]{:S(2)}, u32[]{:S(2)}) async-start(bf16[128,16,256]{0,2,1:T(8,128)(2,1)} %bitcast.1), calls=%async_computation | async-start | bytes 2097152 | tf_op jit(solution)/shard_map/all_to_all | solution.py:56
  33.7 41.2 %all-to-all-start.1 = ((bf16[128,16,256]{2,0,1:T(8,128)(2,1)}), bf16[128,16,256]{2,0,1:T(8,128)(2,1)S(1)}, u32[]{:S(2)}, u32[]{:S(2)}) async-start(bf16[128,16,256]{2,0,1:T(8,128)(2,1)} %bitcast.4), calls=%async_computation.1 | async-start | bytes 2097152 | tf_op jit(solution)/shard_map/all_to_all | solution.py:57
  75.2 56.6 %copy-start.1 = (s32[1,128]{1,0:T(1,128)S(1)}, s32[1,128]{1,0:T(1,128)}, u32[]{:S(2)}) copy-start(s32[1,128]{1,0:T(1,128)} %param.13) | copy-start | bytes 1540
  126.0 29.8 %all-to-all-start.2 = ((bf16[16,2,16384]{2,1,0:T(2,128)(2,1)}), bf16[16,2,16384]{2,1,0:T(2,128)(2,1)S(1)}, u32[]{:S(2)}, u32[]{:S(2)}) async-start(bf16[16,2,16384]{2,1,0:T(2,128)(2,1)} %reshape.308), calls=%async_computation.2 | async-start | bytes 2097152 | tf_op jit(solution)/shard_map/all_to_all | solution.py:66
  155.8 11.8 %all-to-all-start.3 = ((bf16[32,1,8]{2,1,0:T(2,128)(2,1)}), bf16[32,1,8]{2,1,0:T(2,128)(2,1)S(1)}, u32[]{:S(2)}, u32[]{:S(2)}) async-start(bf16[32,1,8]{2,1,0:T(2,128)(2,1)} %all_to_all.61), calls=%async_computation.3 | async-start | bytes 32768 | tf_op jit(solution)/shard_map/all_to_all | solution.py:99
  167.6 52.4 %all-to-all-start.4 = ((bf16[32,8,4096]{2,1,0:T(8,128)(2,1)}), bf16[32,8,4096]{2,1,0:T(8,128)(2,1)S(1)}, u32[]{:S(2)}, u32[]{:S(2)}) async-start(bf16[32,8,4096]{2,1,0:T(8,128)(2,1)} %bitcast.19), calls=%async_computation.4 | async-start | bytes 4194304 | tf_op jit(solution)/shard_map/all_to_all | solution.py:88
  231.7 52.4 %all-to-all-start.5 = ((bf16[32,8,4096]{2,1,0:T(8,128)(2,1)}), bf16[32,8,4096]{2,1,0:T(8,128)(2,1)S(1)}, u32[]{:S(2)}, u32[]{:S(2)}) async-start(bf16[32,8,4096]{2,1,0:T(8,128)(2,1)} %fusion.25), calls=%async_computation.5 | async-start | bytes 4194304 | tf_op jit(solution)/shard_map/all_to_all | solution.py:112
where the time goes:
time: 292 us; the launch traced here: 288 us
  waiting for transfers between devices  132 us (45%)
  starting transfers between devices  35.4 us (12%)
  matrix products  34.3 us (12%)
  blocking collectives  33.3 us (11%)
  local copies, waits for them, and re-layouts  29.4 us (10%)
  other arithmetic  20.5 us (7%)
  loops' own time  2.96 us (1%)
    all_to_all x1, waiting for transfers between devices, local(): lax.all_to_all(send_rows.reshape(devices, capacity, width), ('seq', 'stor...  46.4 us
    all_to_all x1, waiting for transfers between devices, local(): lax.all_to_all(delta.reshape(got_rows.shape), ('seq', 'store'), split_axi...  41.9 us
    all_gather x1, blocking collectives, local(): segments = lax.all_gather(segment_ids, 'seq', axis=1, tiled=True)[0]  33.3 us
    all_to_all x1, waiting for transfers between devices, local(): lax.all_to_all(q_send, 'seq', split_axis=1, concat_axis=0, tiled=True)  21.9 us
    all_to_all x1, waiting for transfers between devices, local(): lax.all_to_all(context.reshape(length, 1, heads_here * HEAD_DIM), 'seq',...  21.8 us
    dot_general x4, matrix products, one_block(): jnp.einsum('qhd,nd->hqn', q_block, key_rows, preferred_element_type=jnp.f...  12.8 us
    dot_general x1, matrix products, local(): jnp.dot(low, adapter_up, preferred_element_type=jnp.float32)  11.6 us
    reduce_sum x4, other arithmetic, one_block(): total = jnp.sum(expo, axis=-1)  10.3 us
  transfers between devices with their start and end apart: 6, of which 4 were waited for; matrix products, arithmetic and copies ran while one was open for 6% of the time, Pallas kernels for 0%

commit v1 on v0

v1 whole, which is shorter than its diff:
```python
import functools

import jax
import jax.numpy as jnp
from jax import lax
from jax.experimental import pallas as pl
from jax.experimental.pallas import tpu as pltpu
from jax.sharding import PartitionSpec as P

HEAD_DIM = 128
HEADS = 32
KV_HEADS = 4
RANK = 64
EXP_DEV = 16
GROUPS = 4
HOPS = 2
SEG_ROWS = 16
MESH = pl.DeviceIdType.MESH


def gather_kernel(n_seq, own_ref, out_ref, local_sem, send_sem, recv_sem):
    per = n_seq // GROUPS
    me = lax.axis_index("seq")
    st = lax.axis_index("store")
    level = me // per
    bits = []
    bit = 2
    while bit < per:
        bits.append(bit)
        bit *= 2
    bits.append(1)

    def flip(b, index=None):
        index = me if index is None else index
        return index + b - 2 * b * ((index // b) % 2)

    barrier = pltpu.get_barrier_semaphore()
    for b in bits:
        pl.semaphore_signal(barrier, inc=1, device_id=(flip(b), st), device_id_type=MESH)

    @pl.when(level < GROUPS - 1)
    def _():
        pl.semaphore_signal(barrier, inc=1, device_id=(me + per, st), device_id_type=MESH)

    @pl.when(level > 0)
    def _():
        pl.semaphore_signal(barrier, inc=1, device_id=(me - per, st), device_id_type=MESH)

    ends = (level < GROUPS - 1).astype(jnp.int32) + (level > 0).astype(jnp.int32)
    pl.semaphore_wait(barrier, len(bits) + ends)

    def remote(source, block, target, sem):
        return pltpu.make_async_remote_copy(
            src_ref=source,
            dst_ref=out_ref.at[block],
            send_sem=send_sem.at[sem],
            recv_sem=recv_sem.at[sem],
            device_id=(target, st),
            device_id_type=MESH,
        )

    def guarded(condition, act):
        if condition is None:
            act()
        else:
            pl.when(condition)(act)

    steps = []
    sem = HOPS
    for hop in range(HOPS + 1):
        masks = [0]
        for b in bits:
            for m in masks:
                steps.append((sem, m, hop, b))
                sem += 1
            masks = masks + [m ^ b for m in masks]

    def column(m):
        index = me
        for b in bits:
            if m & b:
                index = flip(b, index)
        return index

    def at(m, hop):
        return jnp.maximum(column(m) - hop * per, 0)

    def block_ref(m, hop):
        return own_ref if (m == 0 and hop == 0) else out_ref.at[at(m, hop)]

    mine = pltpu.make_async_copy(own_ref, out_ref.at[me], local_sem)
    mine.start()
    up = jnp.minimum(me + per, n_seq - 1)

    def z_copy(hop):
        return remote(block_ref(0, hop), at(0, hop), up, hop)

    def z_arrival(hop):
        return remote(block_ref(0, hop), at(0, hop), up, hop - 1)

    def x_copy(step):
        s, m, hop, b = step
        return remote(block_ref(m, hop), at(m, hop), flip(b), s)

    def x_arrival(step):
        s, m, hop, b = step
        ref = out_ref.at[jnp.maximum(flip(b, column(m)) - hop * per, 0)]
        return pltpu.make_async_remote_copy(
            src_ref=ref, dst_ref=ref, send_sem=send_sem.at[s], recv_sem=recv_sem.at[s],
            device_id=(flip(b), st), device_id_type=MESH,
        )

    z_conditions = [(level < GROUPS - 1) & (level >= hop) for hop in range(HOPS)]
    guarded(z_conditions[0], lambda: z_copy(0).start())
    for hop in range(HOPS + 1):
        condition = None if hop == 0 else level >= hop
        if hop > 0:
            arrived = z_arrival(hop)
            guarded(condition, arrived.wait_recv)
            if hop < HOPS:
                guarded(z_conditions[hop], z_copy(hop).start)
        group = [s for s in steps if s[2] == hop]

        first = [s for s in group if s[1] == 0]

        def begin(first=first):
            for s in first:
                x_copy(s).start()

        guarded(condition, begin)
    for hop in range(HOPS + 1):
        condition = None if hop == 0 else level >= hop
        group = [s for s in steps if s[2] == hop]

        def rest(group=group):
            have = {0}
            waiting = list(group)
            for position, b in enumerate(bits):
                stage = [s for s in waiting if s[3] == b]
                for s in stage:
                    if s[1] != 0:
                        x_copy(s).start()
                for s in stage:
                    x_arrival(s).wait_recv()
            for s in group:
                x_copy(s).wait_send()

        guarded(condition, rest)
    for hop in range(HOPS):
        guarded(z_conditions[hop], z_copy(hop).wait_send)
    mine.wait()


def gather_blocks(block, n_seq):
    per = n_seq // GROUPS
    copies = HOPS + (HOPS + 1) * (per - 1)
    return pl.pallas_call(
        functools.partial(gather_kernel, n_seq),
        out_shape=jax.ShapeDtypeStruct((n_seq,) + block.shape, block.dtype),
        in_specs=[pl.BlockSpec(memory_space=pl.ANY)],
        out_specs=pl.BlockSpec(memory_space=pl.ANY),
        scratch_shapes=[
            pltpu.SemaphoreType.DMA,
            pltpu.SemaphoreType.DMA((copies,)),
            pltpu.SemaphoreType.DMA((copies,)),
        ],
        compiler_params=pltpu.CompilerParams(collective_id=1, has_side_effects=True),
        name="gather_blocks",
    )(block)


def attend_kernel(tok, info_ref, q_ref, k_ref, v_ref, kseg_ref, qseg_ref, place_ref, ctx_ref, send_ref, m_ref, l_ref, acc_ref):
    group = HEADS // KV_HEADS
    me = info_ref[0]
    first = info_ref[1]
    coef = (HEAD_DIM**-0.5) * 1.4426950408889634
    q = jnp.concatenate([q_ref[:, h * HEAD_DIM : (h + 1) * HEAD_DIM] for h in range(group)], axis=0)
    m_ref[...] = jnp.full_like(m_ref, -1e30)
    l_ref[...] = jnp.zeros_like(l_ref)
    acc_ref[...] = jnp.zeros_like(acc_ref)

    @pl.loop(first // 2, me // 2 + 1)
    def _(pair):
        k = k_ref[pl.ds(2 * pair, 2), :tok].reshape(2 * tok, HEAD_DIM)
        v = v_ref[pl.ds(2 * pair, 2), :tok].reshape(2 * tok, HEAD_DIM)
        s = lax.dot_general(k, q, (((1,), (1,)), ((), ())), preferred_element_type=jnp.float32)
        key_pos = 2 * pair * tok + lax.broadcasted_iota(jnp.int32, (2 * tok, tok), 0)
        q_pos = me * tok + lax.broadcasted_iota(jnp.int32, (2 * tok, tok), 1)
        kseg = kseg_ref[pl.ds(2 * pair, 2)].reshape(2 * tok, 1)
        seen = (key_pos <= q_pos) & (kseg == qseg_ref[...])
        bias = jnp.where(seen, 0.0, -1e30).astype(jnp.float32)
        s = s + jnp.concatenate([bias] * group, axis=1)
        m_old = m_ref[...]
        m_new = jnp.maximum(m_old, jnp.max(s, axis=0, keepdims=True))
        alpha = jnp.exp2((m_old - m_new) * coef)
        p = jnp.exp2((s - m_new) * coef)
        m_ref[...] = m_new
        l_ref[...] = l_ref[...] * alpha + jnp.sum(p, axis=0, keepdims=True)
        pv = lax.dot_general(
            v, p.astype(jnp.bfloat16), (((0,), (0,)), ((), ())), preferred_element_type=jnp.float32
        )
        acc_ref[...] = acc_ref[...] * alpha + pv

    out = acc_ref[...] / l_ref[...]
    for h in range(group):
        ctx_ref[:, h * HEAD_DIM : (h + 1) * HEAD_DIM] = out[:, h * tok : (h + 1) * tok].T.astype(jnp.bfloat16)
    send_ref[...] = jnp.dot(place_ref[...], ctx_ref[...], preferred_element_type=jnp.float32).astype(jnp.bfloat16)


def attend(info, queries, blocks, kseg, qseg, place):
    tok, width = queries.shape
    n_seq, rows, _ = blocks.shape
    slots = place.shape[0]
    part = width // KV_HEADS
    cols = tok * (HEADS // KV_HEADS)
    return pl.pallas_call(
        functools.partial(attend_kernel, tok),
        out_shape=(
            jax.ShapeDtypeStruct((tok, width), jnp.bfloat16),
            jax.ShapeDtypeStruct((slots, width), jnp.bfloat16),
        ),
        grid=(KV_HEADS,),
        in_specs=[
            pl.BlockSpec(memory_space=pltpu.SMEM),
            pl.BlockSpec((tok, part), lambda g: (0, g)),
            pl.BlockSpec((n_seq, rows, HEAD_DIM), lambda g: (0, 0, g)),
            pl.BlockSpec((n_seq, rows, HEAD_DIM), lambda g: (0, 0, KV_HEADS + g)),
            pl.BlockSpec((n_seq, tok, 1), lambda g: (0, 0, 0)),
            pl.BlockSpec((1, tok), lambda g: (0, 0)),
            pl.BlockSpec((slots, tok), lambda g: (0, 0)),
        ],
        out_specs=(
            pl.BlockSpec((tok, part), lambda g: (0, g)),
            pl.BlockSpec((slots, part), lambda g: (0, g)),
        ),
        scratch_shapes=[
            pltpu.VMEM((1, cols), jnp.float32),
            pltpu.VMEM((1, cols), jnp.float32),
            pltpu.VMEM((HEAD_DIM, cols), jnp.float32),
        ],
        compiler_params=pltpu.CompilerParams(vmem_limit_bytes=48 << 20),
        name="attend",
    )(info, queries, blocks, blocks, kseg, qseg, place)


def local(queries, keys, values, segment_ids, route_ids, adapter_down, adapter_up):
    n_seq = lax.axis_size("seq")
    n_store = lax.axis_size("store")
    tok = queries.shape[1]
    width = queries.shape[2]
    me = lax.axis_index("seq")
    seg = segment_ids[0].astype(jnp.bfloat16)
    seg_row = jnp.pad(seg[None, :], ((0, SEG_ROWS - 1), (0, keys.shape[2] * 2 - tok)))
    own = jnp.concatenate([jnp.concatenate([keys[0], values[0]], axis=1), seg_row], axis=0)
    blocks = gather_blocks(own, n_seq)

    devices = n_seq * n_store
    capacity = max(2, 2 * tok // devices)
    chosen = route_ids[0]
    owners = chosen // EXP_DEV
    one_hot = (owners[:, None] == jnp.arange(devices, dtype=jnp.int32)[None, :]).astype(jnp.bfloat16)
    lower = jnp.tril(jnp.ones((tok, tok), jnp.bfloat16))
    counts = jnp.dot(lower, one_hot, preferred_element_type=jnp.float32)
    slot_of = jnp.sum(counts * one_hot.astype(jnp.float32), axis=1).astype(jnp.int32) - 1
    placed = owners * capacity + slot_of
    hits = jnp.arange(devices * capacity, dtype=jnp.int32)[:, None] == placed[None, :]
    place = hits.astype(jnp.bfloat16)
    send_tags = (
        jnp.sum(jnp.where(hits, (chosen % EXP_DEV + 1).astype(jnp.float32)[None, :], 0.0), axis=1) - 1.0
    ).astype(jnp.bfloat16)
    tags = lax.all_to_all(
        send_tags.reshape(devices, capacity), ("seq", "store"), split_axis=0, concat_axis=0, tiled=True
    ).reshape(-1, 1)

    kseg = blocks[:, tok, :tok].astype(jnp.float32)
    qseg = seg.astype(jnp.float32)
    index = jnp.arange(n_seq, dtype=jnp.int32)
    wanted = (index >= me - n_seq // HOPS) & (index < me) & (kseg[:, tok - 1] >= qseg[0])
    first = jnp.min(jnp.where(wanted, index, me))
    info = jnp.stack([me, first]).astype(jnp.int32)
    tok_ctx, send_rows = attend(info, queries[0], blocks, kseg[:, :, None], qseg[None, :], place)

    flat_rows = lax.all_to_all(
        send_rows.reshape(devices, capacity, width), ("seq", "store"), split_axis=0, concat_axis=0, tiled=True
    ).reshape(-1, width)
    low = jnp.dot(flat_rows, adapter_down, preferred_element_type=jnp.float32)
    lane_owner = (jnp.arange(low.shape[1], dtype=jnp.int32) // RANK).astype(jnp.float32)
    low = jnp.where(tags.astype(jnp.float32) == lane_owner[None, :], low, 0.0).astype(jnp.bfloat16)
    delta = jnp.dot(low, adapter_up, preferred_element_type=jnp.float32).astype(jnp.bfloat16)
    answer = lax.all_to_all(
        delta.reshape(devices, capacity, width), ("seq", "store"), split_axis=0, concat_axis=0, tiled=True
    ).reshape(-1, width)
    delta_rows = lax.dot_general(place, answer, (((0,), (0,)), ((), ())), preferred_element_type=jnp.float32)
    return (tok_ctx.astype(jnp.float32) + delta_rows).astype(jnp.bfloat16)[None]


def solution(mesh):
    return jax.shard_map(
        local,
        mesh=mesh,
        in_specs=(
            P("store", "seq", None),
            P("store", "seq", None),
            P("store", "seq", None),
            P("store", "seq"),
            P("store", "seq"),
            P(None, ("seq", "store")),
            P(("seq", "store"), None),
        ),
        out_specs=P("store", "seq", None),
        check_vma=False,
    )
```

time: 292 us -> 179 us (0.61)
  waiting for transfers between devices: 132 us -> 46.5 us
  Pallas kernels: 0 us -> 35.5 us
  local copies, waits for them, and re-layouts: 29.4 us -> 1.16 us
  matrix products: 34.3 us -> 13.8 us
  blocking collectives: 33.3 us -> 52.6 us
  starting transfers between devices: 35.4 us -> 19.7 us
  other arithmetic: 20.5 us -> 6.1 us
  loops' own time: 2.96 us -> 0 us
    all_to_all x4 -> x0, waiting for transfers between devices: 85.6 us -> none  [the longest x1 41.9 us: local(): lax.all_to_all(delta.reshape(got_rows.shape), ('seq', 'store'), split_axi...]
    all_to_all x0 -> x1, blocking collectives: none -> 52.6 us  [local(): lax.all_to_all(delta.reshape(devices, capacity, width), ('seq', 'store'),...]
    pallas_call x0 -> x2, Pallas kernels: none -> 35.5 us  [the longest x1 25.4 us: gather_blocks(): pl.pallas_call(functools.partial(gather_kernel, n_seq), out_shape=jax.Sha...]
    all_gather x1 -> x0, blocking collectives: 33.3 us -> none  [local(): segments = lax.all_gather(segment_ids, 'seq', axis=1, tiled=True)[0]]
    all_to_all x4 -> x0, starting transfers between devices: 23.9 us -> none  [the longest x1 6.33 us: local(): lax.all_to_all(q_send, 'seq', split_axis=1, concat_axis=0, tiled=True)]
    dot_general x8 -> x2, matrix products: 22.7 us -> 1.63 us  [the longest x1 1.48 us: local(): lax.dot_general(place, answer, (((0,), (0,)), ((), ())), preferred_elemen...]
    reduce_sum x5 -> x1, other arithmetic: 10.4 us -> 0.11 us  [local(): jnp.sum(jnp.where(hits, (chosen % EXP_DEV + 1).astype(jnp.float32)[None,...]
    all_to_all x1, starting transfers between devices: 5.83 us -> 13.5 us  [local(): lax.all_to_all(send_rows.reshape(devices, capacity, width), ('seq', 'stor...]
  transfers between devices with their start and end apart: 6 -> 2, of which waited for: 4 -> 1; matrix products, arithmetic and copies ran while one was open for 6% -> 3% of each run, Pallas kernels for 0% -> 20%
where the time goes in v1:
time: 179 us; the launch traced here: 176 us
  blocking collectives  52.6 us (29%)
  waiting for transfers between devices  46.5 us (26%)
  Pallas kernels  35.5 us (20%)
  starting transfers between devices  19.7 us (11%)
  matrix products  13.8 us (8%)
  other arithmetic  6.1 us (3%)
    all_to_all x1, blocking collectives, local(): lax.all_to_all(delta.reshape(devices, capacity, width), ('seq', 'store'),...  52.6 us
    all_to_all x1, waiting for transfers between devices, local(): lax.all_to_all(send_rows.reshape(devices, capacity, width), ('seq', 'stor...  46.5 us
    pallas_call x1, Pallas kernels, gather_blocks(): pl.pallas_call(functools.partial(gather_kernel, n_seq), out_shape=jax.Sha...  25.4 us
    all_to_all x1, starting transfers between devices, local(): lax.all_to_all(send_rows.reshape(devices, capacity, width), ('seq', 'stor...  13.5 us
    dot_general x1, matrix products, local(): jnp.dot(low, adapter_up, preferred_element_type=jnp.float32)  12.2 us
    pallas_call x1, Pallas kernels, attend(): pl.pallas_call(functools.partial(attend_kernel, tok), out_shape=(jax.Shap...  10.1 us
    all_to_all x1, starting transfers between devices, local(): lax.all_to_all(send_tags.reshape(devices, capacity), ('seq', 'store'), sp...  6.17 us
  transfers between devices with their start and end apart: 2, of which 1 were waited for; matrix products, arithmetic and copies ran while one was open for 3% of the time, Pallas kernels for 20%

profile of v1, /device:TPU:27, one launch (start us, length us, event | category | flops | bytes accessed | tf_op | source)
XLA Modules:
  0.0 175.5 jit_solution(4131006045313446499)
XLA Ops:
  0.0 0.7 and_select_fusion.1
  0.7 0.2 fusion.12
  0.8 0.7 fusion.35
  1.5 0.1 select_reduce_fusion
  1.6 0.7 convert_element_type.118
  2.3 6.2 %all-to-all-start = ((bf16[32,1,8]{2,1,0:T(2,128)(2,1)}), bf16[32,1,8]{2,1,0:T(2,128)(2,1)S(1)}, u32[]{:S(2)}, u32[]{:S(2)}) async-start(bf16[32,1,8]{2,1,0:T(2,128)(2,1)} %convert_element_type.118), calls=%async_computation | async-start | bytes 32768 | tf_op jit(solution)/shard_map/all_to_all | solution.py:271
  8.5 0.7 convert_convert_fusion
  9.2 1.7 fusion.19.own_ref
  10.9 0.0 copy-start
  10.9 25.4 %gather_blocks.1.k_ref.v_ref = bf16[16,144,1024]{2,1,0:T(8,128)(2,1)} custom-call(bf16[144,1024]{1,0:T(8,128)(2,1)} %fusion.19.own_ref), custom_call_target="tpu_custom_call" | custom-call | tf_op jit(solution)/shard_map/gather_blocks/pallas_call | solution.py:157
  36.3 0.8 slice_convert_fusion
  37.2 0.2 fusion.28
  37.3 0.6 fusion.37
  38.0 0.6 pad_add_fusion.info_ref
  38.6 0.4 copy.11.kseg_ref
  38.9 0.0 copy-done
  39.0 10.1 %attend.1 = (bf16[128,4096]{1,0:T(8,128)(2,1)S(1)}, bf16[256,4096]{1,0:T(8,128)(2,1)}) custom-call(s32[2]{0:T(128)S(1)} %pad_add_fusion.info_ref, bf16[128,4096]{1,0:T(8,128)(2,1)S(1)} %bitcast.47, bf16[16,144,1024]{2,1,0:T(8,128)(2,1)} %gather_blocks.1.k_ref.v_ref, bf16[16,144,1024]{2,1,0:T(8,128)(2,1)} %gather_blocks.1.k_ref.v_ref, ...), custom_call_target="tpu_custom_call" | custom-call | tf_op jit(solution)/shard_map/attend/pallas_call | solution.py:216
  49.1 0.0 all-to-all-done
  49.1 13.5 %all-to-all-start.1 = ((bf16[32,8,4096]{2,1,0:T(8,128)(2,1)}), bf16[32,8,4096]{2,1,0:T(8,128)(2,1)}, u32[]{:S(2)}, u32[]{:S(2)}) async-start(bf16[32,8,4096]{2,1,0:T(8,128)(2,1)} %bitcast.11), calls=%async_computation.1 | async-start | bytes 4194304 | tf_op jit(solution)/shard_map/all_to_all | solution.py:283
  62.6 0.1 convert_reduce_fusion
  62.7 0.1 reshape.124
  62.7 46.5 %all-to-all-done.1 = bf16[32,8,4096]{2,1,0:T(8,128)(2,1)} async-done(((bf16[32,8,4096]{2,1,0:T(8,128)(2,1)}), bf16[32,8,4096]{2,1,0:T(8,128)(2,1)}, u32[]{:S(2)}, u32[]{:S(2)}) %all-to-all-start.1) | async-done | bytes 2097184 | tf_op jit(solution)/shard_map/all_to_all | solution.py:283
  109.2 12.2 %fusion = bf16[32,8,4096]{2,1,0:T(8,128)(2,1)} fusion(bf16[1024,4096]{1,0:T(8,128)(2,1)} %param.13, bf16[4096,1024]{1,0:T(8,128)(2,1)} %param.12, bf16[32,8,4096]{2,1,0:T(8,128)(2,1)} %all-to-all-done.1, f32[1024]{0:T(1024)S(1)} %fusion.29, f32[256]{0:T(256)S(1)} %reshape.124), kind=kOutput, calls=%fused_computation.1 | convolution fusion | flops 4296802304 | bytes 20976640 | tf_op jit(solution)/shard_map/dot_general | solution.py:289
  121.4 52.6 %all_to_all.16 = bf16[32,8,4096]{2,1,0:T(8,128)(2,1)S(1)} all-to-all(bf16[32,8,4096]{2,1,0:T(8,128)(2,1)} %fusion), channel_id=1, replica_groups=mesh['seq'=16,'store'=2] {'seq','store'}, dimensions={0} | all-to-all | bytes 4194304 | tf_op jit(solution)/shard_map/all_to_all | solution.py:290
  174.0 1.5 fusion.2
  (4 shorter events, 0.0 us)
Async XLA Ops:
  2.3 46.7 %all-to-all-start = ((bf16[32,1,8]{2,1,0:T(2,128)(2,1)}), bf16[32,1,8]{2,1,0:T(2,128)(2,1)S(1)}, u32[]{:S(2)}, u32[]{:S(2)}) async-start(bf16[32,1,8]{2,1,0:T(2,128)(2,1)} %convert_element_type.118), calls=%async_computation | async-start | bytes 32768 | tf_op jit(solution)/shard_map/all_to_all | solution.py:271
  10.9 28.0 %copy-start = (bf16[1,128,4096]{2,1,0:T(8,128)(2,1)S(1)}, bf16[1,128,4096]{2,1,0:T(8,128)(2,1)}, u32[]{:S(2)}) copy-start(bf16[1,128,4096]{2,1,0:T(8,128)(2,1)} %param.7) | copy-start | bytes 3145732
  49.1 60.2 %all-to-all-start.1 = ((bf16[32,8,4096]{2,1,0:T(8,128)(2,1)}), bf16[32,8,4096]{2,1,0:T(8,128)(2,1)}, u32[]{:S(2)}, u32[]{:S(2)}) async-start(bf16[32,8,4096]{2,1,0:T(8,128)(2,1)} %bitcast.11), calls=%async_computation.1 | async-start | bytes 4194304 | tf_op jit(solution)/shard_map/all_to_all | solution.py:283

commit v2 on v1

--- a/solution.py
+++ b/solution.py
@@ -169,86 +169,215 @@
     )(block)
 
 
-def attend_kernel(tok, info_ref, q_ref, k_ref, v_ref, kseg_ref, qseg_ref, place_ref, ctx_ref, send_ref, m_ref, l_ref, acc_ref):
+def routed_kernel(
+    n_store, devices, cap,
+    q_ref, kv_ref, kseg_ref, qseg_ref, place_ref, tags_ref, down_hbm, up_hbm,
+    out_ref,
+    weight_ref, ctx_ref, m_ref, l_ref, acc_ref, send_ref, got_ref, ans_ref, tag_ref, total_ref, low_ref,
+    load_sem, send_sem, recv_sem,
+):
+    tok = q_ref.shape[0]
+    n_seq = kv_ref.shape[0]
     group = HEADS // KV_HEADS
-    me = info_ref[0]
-    first = info_ref[1]
+    part = group * HEAD_DIM
+    split = SEG_ROWS // cap
+    piece = part // split
+    slots = devices * cap
+    packed = devices * SEG_ROWS
+    me = lax.axis_index("seq")
+    flat = me * n_store + lax.axis_index("store")
     coef = (HEAD_DIM**-0.5) * 1.4426950408889634
-    q = jnp.concatenate([q_ref[:, h * HEAD_DIM : (h + 1) * HEAD_DIM] for h in range(group)], axis=0)
-    m_ref[...] = jnp.full_like(m_ref, -1e30)
-    l_ref[...] = jnp.zeros_like(l_ref)
-    acc_ref[...] = jnp.zeros_like(acc_ref)
-
-    @pl.loop(first // 2, me // 2 + 1)
-    def _(pair):
-        k = k_ref[pl.ds(2 * pair, 2), :tok].reshape(2 * tok, HEAD_DIM)
-        v = v_ref[pl.ds(2 * pair, 2), :tok].reshape(2 * tok, HEAD_DIM)
-        s = lax.dot_general(k, q, (((1,), (1,)), ((), ())), preferred_element_type=jnp.float32)
-        key_pos = 2 * pair * tok + lax.broadcasted_iota(jnp.int32, (2 * tok, tok), 0)
-        q_pos = me * tok + lax.broadcasted_iota(jnp.int32, (2 * tok, tok), 1)
-        kseg = kseg_ref[pl.ds(2 * pair, 2)].reshape(2 * tok, 1)
-        seen = (key_pos <= q_pos) & (kseg == qseg_ref[...])
-        bias = jnp.where(seen, 0.0, -1e30).astype(jnp.float32)
-        s = s + jnp.concatenate([bias] * group, axis=1)
-        m_old = m_ref[...]
-        m_new = jnp.maximum(m_old, jnp.max(s, axis=0, keepdims=True))
-        alpha = jnp.exp2((m_old - m_new) * coef)
-        p = jnp.exp2((s - m_new) * coef)
-        m_ref[...] = m_new
-        l_ref[...] = l_ref[...] * alpha + jnp.sum(p, axis=0, keepdims=True)
-        pv = lax.dot_general(
-            v, p.astype(jnp.bfloat16), (((0,), (0,)), ((), ())), preferred_element_type=jnp.float32
+
+    up_at = weight_ref.shape[0] - 1
+
+    def load_down(g):
+        rows = pl.ds(pl.multiple_of(g * part, part), part)
+        return pltpu.make_async_copy(down_hbm.at[rows], weight_ref.at[0, g], load_sem.at[g])
+
+    def load_up(g):
+        cols = pl.ds(pl.multiple_of(g * part, part), part)
+        return pltpu.make_async_copy(up_hbm.at[:, cols], weight_ref.at[up_at, g], load_sem.at[KV_HEADS + g])
+
+    @pl.loop(0, KV_HEADS)
+    def _(g):
+        load_down(g).start()
+        if up_at:
+            load_up(g).start()
+
+    barrier = pltpu.get_barrier_semaphore()
+
+    @pl.loop(1, devices)
+    def _(p):
+        peer = (flat + p) % devices
+        pl.semaphore_signal(barrier, inc=1, device_id=(peer // n_store, peer % n_store), device_id_type=MESH)
+
+    pl.semaphore_wait(barrier, devices - 1)
+
+    def exchange(source, target, sem):
+        @pl.loop(1, devices)
+        def _(p):
+            peer = (flat + p) % devices
+            pltpu.make_async_remote_copy(
+                src_ref=source.at[peer], dst_ref=target.at[flat], send_sem=send_sem.at[sem], recv_sem=recv_sem.at[sem],
+                device_id=(peer // n_store, peer % n_store), device_id_type=MESH,
+            ).start()
+
+    def all_of(source, target, sem):
+        others = pl.ds(0, devices - 1)
+        return pltpu.make_async_remote_copy(
+            src_ref=source.at[others], dst_ref=target.at[others], send_sem=send_sem.at[sem], recv_sem=recv_sem.at[sem],
+            device_id=((me + 1) % n_seq, lax.axis_index("store")), device_id_type=MESH,
         )
-        acc_ref[...] = acc_ref[...] * alpha + pv
-
-    out = acc_ref[...] / l_ref[...]
-    for h in range(group):
-        ctx_ref[:, h * HEAD_DIM : (h + 1) * HEAD_DIM] = out[:, h * tok : (h + 1) * tok].T.astype(jnp.bfloat16)
-    send_ref[...] = jnp.dot(place_ref[...], ctx_ref[...], preferred_element_type=jnp.float32).astype(jnp.bfloat16)
-
-
-def attend(info, queries, blocks, kseg, qseg, place):
+
+    exchange(tags_ref, tag_ref, 2 * KV_HEADS)
+    tag_ref[flat] = tags_ref[flat]
+
+    @pl.loop(0, KV_HEADS)
+    def _(g):
+        start = pl.multiple_of(g * part, part)
+        q_all = q_ref[:, pl.ds(start, part)]
+        q = jnp.concatenate([q_all[:, h * HEAD_DIM : (h + 1) * HEAD_DIM] for h in range(group)], axis=0)
+        m_ref[...] = jnp.full_like(m_ref, -1e30)
+        l_ref[...] = jnp.zeros_like(l_ref)
+        acc_ref[...] = jnp.zeros_like(acc_ref)
+        k_cols = pl.ds(pl.multiple_of(g * HEAD_DIM, HEAD_DIM), HEAD_DIM)
+        v_cols = pl.ds(pl.multiple_of((KV_HEADS + g) * HEAD_DIM, HEAD_DIM), HEAD_DIM)
+
+        @pl.loop(jnp.maximum(me - n_seq // HOPS, 0) // 2, me // 2 + 1)
+        def _(pair):
+            k = kv_ref[pl.ds(2 * pair, 2), :tok, k_cols].reshape(2 * tok, HEAD_DIM)
+            v = kv_ref[pl.ds(2 * pair, 2), :tok, v_cols].reshape(2 * tok, HEAD_DIM)
+            s = lax.dot_general(k, q, (((1,), (1,)), ((), ())), preferred_element_type=jnp.float32)
+            key_pos = 2 * pair * tok + lax.broadcasted_iota(jnp.int32, (2 * tok, tok), 0)
+            q_pos = me * tok + lax.broadcasted_iota(jnp.int32, (2 * tok, tok), 1)
+            kseg = kseg_ref[pl.ds(2 * pair, 2)].reshape(2 * tok, 1)
+            seen = (key_pos <= q_pos) & (kseg == qseg_ref[...])
+            bias = jnp.where(seen, 0.0, -1e30).astype(jnp.float32)
+            s = s + jnp.concatenate([bias] * group, axis=1)
+            m_old = m_ref[...]
+            m_new = jnp.maximum(m_old, jnp.max(s, axis=0, keepdims=True))
+            alpha = jnp.exp2((m_old - m_new) * coef)
+            p = jnp.exp2((s - m_new) * coef)
+            m_ref[...] = m_new
+            l_ref[...] = l_ref[...] * alpha + jnp.sum(p, axis=0, keepdims=True)
+            pv = lax.dot_general(
+                v, p.astype(jnp.bfloat16), (((0,), (0,)), ((), ())), preferred_element_type=jnp.float32
+            )
+            acc_ref[...] = acc_ref[...] * alpha + pv
+
+        out = acc_ref[...] / l_ref[...]
+        ctx = jnp.concatenate([out[:, h * tok : (h + 1) * tok].T for h in range(group)], axis=1).astype(jnp.bfloat16)
+        ctx_ref[:, pl.ds(start, part)] = ctx
+        stacked = jnp.concatenate([ctx[:, i * piece : (i + 1) * piece] for i in range(split)], axis=0)
+        rows = jnp.dot(place_ref[...], stacked, preferred_element_type=jnp.float32).astype(jnp.bfloat16)
+        send_ref[g] = rows.reshape(devices, SEG_ROWS, piece)
+        exchange(send_ref.at[g], got_ref.at[g], g)
+        got_ref[g, flat] = send_ref[g, flat]
+
+    def chosen_rows(i):
+        row = lax.broadcasted_iota(jnp.int32, (slots, 1), 0)
+        column = lax.broadcasted_iota(jnp.int32, (1, packed), 1)
+        wanted = (row // cap) * SEG_ROWS + i * cap + row % cap
+        return jnp.where(column == wanted, 1.0, 0.0).astype(jnp.bfloat16)
+
+    total_ref[...] = jnp.zeros_like(total_ref)
+    all_of(tags_ref, tag_ref, 2 * KV_HEADS).wait()
+
+    @pl.loop(0, KV_HEADS)
+    def _(g):
+        all_of(send_ref.at[g], got_ref.at[g], g).wait_recv()
+        load_down(g).wait()
+        got = got_ref[g].reshape(packed, piece)
+        for i in range(split):
+            rows = jnp.dot(chosen_rows(i), got, preferred_element_type=jnp.float32).astype(jnp.bfloat16)
+            total_ref[...] += jnp.dot(rows, weight_ref[0, g, pl.ds(i * piece, piece)], preferred_element_type=jnp.float32)
+
+    tags = jnp.dot(chosen_rows(0), tag_ref[...].reshape(packed, HEAD_DIM), preferred_element_type=jnp.float32)
+    held = total_ref.shape[1]
+    lane = lax.broadcasted_iota(jnp.int32, (slots, held), 1) // RANK + 1
+    tags = jnp.concatenate([tags] * (held // HEAD_DIM), axis=1)
+    low_ref[...] = jnp.where(tags == lane.astype(jnp.float32), total_ref[...], 0.0).astype(jnp.bfloat16)
+    if not up_at:
+
+        @pl.loop(0, KV_HEADS)
+        def _(g):
+            load_up(g).start()
+
+    @pl.loop(0, KV_HEADS)
+    def _(g):
+        load_up(g).wait()
+        delta = jnp.dot(low_ref[...], weight_ref[up_at, g], preferred_element_type=jnp.float32).astype(jnp.bfloat16)
+        rows = jnp.zeros((packed, piece), jnp.float32)
+        for i in range(split):
+            rows += lax.dot_general(
+                chosen_rows(i), delta[:, i * piece : (i + 1) * piece], (((0,), (0,)), ((), ())),
+                preferred_element_type=jnp.float32,
+            )
+        all_of(send_ref.at[g], got_ref.at[g], g).wait_send()
+        send_ref[g] = rows.astype(jnp.bfloat16).reshape(devices, SEG_ROWS, piece)
+        exchange(send_ref.at[g], ans_ref.at[g], KV_HEADS + g)
+        ans_ref[g, flat] = send_ref[g, flat]
+
+    @pl.loop(0, KV_HEADS)
+    def _(g):
+        all_of(send_ref.at[g], ans_ref.at[g], KV_HEADS + g).wait_recv()
+        rows = ans_ref[g].reshape(packed, piece)
+        delta = jnp.concatenate(
+            [
+                lax.dot_general(
+                    place_ref[:, i * tok : (i + 1) * tok], rows, (((0,), (0,)), ((), ())),
+                    preferred_element_type=jnp.float32,
+                )
+                for i in range(split)
+            ],
+            axis=1,
+        )
+        cols = pl.ds(pl.multiple_of(g * part, part), part)
+        out_ref[:, cols] = (ctx_ref[:, cols].astype(jnp.float32) + delta).astype(jnp.bfloat16)
+
+    @pl.loop(0, KV_HEADS)
+    def _(g):
+        all_of(send_ref.at[g], ans_ref.at[g], KV_HEADS + g).wait_send()
+
+
+def routed(n_store, devices, cap, queries, blocks, kseg, qseg, place, tags, down, up):
     tok, width = queries.shape
-    n_seq, rows, _ = blocks.shape
-    slots = place.shape[0]
     part = width // KV_HEADS
+    held = down.shape[1]
     cols = tok * (HEADS // KV_HEADS)
+    wire = (KV_HEADS, devices, SEG_ROWS, part * cap // SEG_ROWS)
+    vmem = pl.BlockSpec(memory_space=pltpu.VMEM)
+    hbm = pl.BlockSpec(memory_space=pl.ANY)
     return pl.pallas_call(
-        functools.partial(attend_kernel, tok),
-        out_shape=(
-            jax.ShapeDtypeStruct((tok, width), jnp.bfloat16),
-            jax.ShapeDtypeStruct((slots, width), jnp.bfloat16),
-        ),
-        grid=(KV_HEADS,),
-        in_specs=[
-            pl.BlockSpec(memory_space=pltpu.SMEM),
-            pl.BlockSpec((tok, part), lambda g: (0, g)),
-            pl.BlockSpec((n_seq, rows, HEAD_DIM), lambda g: (0, 0, g)),
-            pl.BlockSpec((n_seq, rows, HEAD_DIM), lambda g: (0, 0, KV_HEADS + g)),
-            pl.BlockSpec((n_seq, tok, 1), lambda g: (0, 0, 0)),
-            pl.BlockSpec((1, tok), lambda g: (0, 0)),
-            pl.BlockSpec((slots, tok), lambda g: (0, 0)),
-        ],
-        out_specs=(
-            pl.BlockSpec((tok, part), lambda g: (0, g)),
-            pl.BlockSpec((slots, part), lambda g: (0, g)),
-        ),
+        functools.partial(routed_kernel, n_store, devices, cap),
+        out_shape=jax.ShapeDtypeStruct((tok, width), jnp.bfloat16),
+        in_specs=[vmem] * 6 + [hbm] * 2,
+        out_specs=vmem,
         scratch_shapes=[
+            pltpu.VMEM((2 if devices <= 32 else 1, KV_HEADS, part, held), jnp.bfloat16),
+            pltpu.VMEM((tok, width), jnp.bfloat16),
             pltpu.VMEM((1, cols), jnp.float32),
             pltpu.VMEM((1, cols), jnp.float32),
             pltpu.VMEM((HEAD_DIM, cols), jnp.float32),
+            pltpu.VMEM(wire, jnp.bfloat16),
+            pltpu.VMEM(wire, jnp.bfloat16),
+            pltpu.VMEM(wire, jnp.bfloat16),
+            pltpu.VMEM(tags.shape, jnp.bfloat16),
+            pltpu.VMEM((devices * cap, held), jnp.float32),
+            pltpu.VMEM((devices * cap, held), jnp.bfloat16),
+            pltpu.SemaphoreType.DMA((2 * KV_HEADS,)),
+            pltpu.SemaphoreType.DMA((2 * KV_HEADS + 1,)),
+            pltpu.SemaphoreType.DMA((2 * KV_HEADS + 1,)),
         ],
-        compiler_params=pltpu.CompilerParams(vmem_limit_bytes=48 << 20),
-        name="attend",
-    )(info, queries, blocks, blocks, kseg, qseg, place)
+        compiler_params=pltpu.CompilerParams(collective_id=2, has_side_effects=True, vmem_limit_bytes=62 << 20),
+        name="routed",
+    )(queries, blocks, kseg, qseg, place, tags, down, up)
 
 
 def local(queries, keys, values, segment_ids, route_ids, adapter_down, adapter_up):
     n_seq = lax.axis_size("seq")
     n_store = lax.axis_size("store")
     tok = queries.shape[1]
-    width = queries.shape[2]
-    me = lax.axis_index("seq")
     seg = segment_ids[0].astype(jnp.bfloat16)
     seg_row = jnp.pad(seg[None, :], ((0, SEG_ROWS - 1), (0, keys.shape[2] * 2 - tok)))
     own = jnp.concatenate([jnp.concatenate([keys[0], values[0]], axis=1), seg_row], axis=0)
@@ -256,42 +385,27 @@
 
     devices = n_seq * n_store
     capacity = max(2, 2 * tok // devices)
+    split = SEG_ROWS // capacity
     chosen = route_ids[0]
     owners = chosen // EXP_DEV
     one_hot = (owners[:, None] == jnp.arange(devices, dtype=jnp.int32)[None, :]).astype(jnp.bfloat16)
     lower = jnp.tril(jnp.ones((tok, tok), jnp.bfloat16))
     counts = jnp.dot(lower, one_hot, preferred_element_type=jnp.float32)
     slot_of = jnp.sum(counts * one_hot.astype(jnp.float32), axis=1).astype(jnp.int32) - 1
-    placed = owners * capacity + slot_of
-    hits = jnp.arange(devices * capacity, dtype=jnp.int32)[:, None] == placed[None, :]
-    place = hits.astype(jnp.bfloat16)
-    send_tags = (
-        jnp.sum(jnp.where(hits, (chosen % EXP_DEV + 1).astype(jnp.float32)[None, :], 0.0), axis=1) - 1.0
+    placed = owners * SEG_ROWS + slot_of
+    packed = jnp.arange(devices * SEG_ROWS, dtype=jnp.int32)[:, None]
+    place = (packed == jnp.concatenate([placed + i * capacity for i in range(split)])[None, :]).astype(jnp.bfloat16)
+    names = (chosen % EXP_DEV + 1).astype(jnp.bfloat16)
+    tags = jnp.dot(
+        place[:, :tok], jnp.broadcast_to(names[:, None], (tok, HEAD_DIM)), preferred_element_type=jnp.float32
     ).astype(jnp.bfloat16)
-    tags = lax.all_to_all(
-        send_tags.reshape(devices, capacity), ("seq", "store"), split_axis=0, concat_axis=0, tiled=True
-    ).reshape(-1, 1)
-
-    kseg = blocks[:, tok, :tok].astype(jnp.float32)
-    qseg = seg.astype(jnp.float32)
-    index = jnp.arange(n_seq, dtype=jnp.int32)
-    wanted = (index >= me - n_seq // HOPS) & (index < me) & (kseg[:, tok - 1] >= qseg[0])
-    first = jnp.min(jnp.where(wanted, index, me))
-    info = jnp.stack([me, first]).astype(jnp.int32)
-    tok_ctx, send_rows = attend(info, queries[0], blocks, kseg[:, :, None], qseg[None, :], place)
-
-    flat_rows = lax.all_to_all(
-        send_rows.reshape(devices, capacity, width), ("seq", "store"), split_axis=0, concat_axis=0, tiled=True
-    ).reshape(-1, width)
-    low = jnp.dot(flat_rows, adapter_down, preferred_element_type=jnp.float32)
-    lane_owner = (jnp.arange(low.shape[1], dtype=jnp.int32) // RANK).astype(jnp.float32)
-    low = jnp.where(tags.astype(jnp.float32) == lane_owner[None, :], low, 0.0).astype(jnp.bfloat16)
-    delta = jnp.dot(low, adapter_up, preferred_element_type=jnp.float32).astype(jnp.bfloat16)
-    answer = lax.all_to_all(
-        delta.reshape(devices, capacity, width), ("seq", "store"), split_axis=0, concat_axis=0, tiled=True
-    ).reshape(-1, width)
-    delta_rows = lax.dot_general(place, answer, (((0,), (0,)), ((), ())), preferred_element_type=jnp.float32)
-    return (tok_ctx.astype(jnp.float32) + delta_rows).astype(jnp.bfloat16)[None]
+    tags = tags.reshape(devices, SEG_ROWS, HEAD_DIM)
+
+    kseg = blocks[:, tok, :tok].astype(jnp.float32)[:, :, None]
+    qseg = seg.astype(jnp.float32)[None, :]
+    return routed(
+        n_store, devices, capacity, queries[0], blocks, kseg, qseg, place, tags, adapter_down, adapter_up
+    )[None]
 
 
 def solution(mesh):

time: 179 us -> 144 us (0.80); the launches traced: 176 us -> 144 us
  Pallas kernels: 35.5 us -> 134 us
  blocking collectives: 52.6 us -> 0 us
  waiting for transfers between devices: 46.5 us -> 0 us
  starting transfers between devices: 19.7 us -> 0 us
  matrix products: 13.8 us -> 1.06 us
  local copies, waits for them, and re-layouts: 1.16 us -> 3.64 us
    pallas_call x1, Pallas kernels: 10.1 us -> 110 us  [routed(): pl.pallas_call(functools.partial(routed_kernel, n_store, devices, cap), o...]
    all_to_all x1 -> x0, blocking collectives: 52.6 us -> none  [local(): lax.all_to_all(delta.reshape(devices, capacity, width), ('seq', 'store'),...]
    all_to_all x2 -> x0, waiting for transfers between devices: 46.5 us -> none  [the longest x1 46.5 us: local(): lax.all_to_all(send_rows.reshape(devices, capacity, width), ('seq', 'stor...]
    all_to_all x2 -> x0, starting transfers between devices: 19.7 us -> none  [the longest x1 13.5 us: local(): lax.all_to_all(send_rows.reshape(devices, capacity, width), ('seq', 'stor...]
    dot_general x2 -> x1, matrix products: 13.6 us -> 0.91 us  [local(): jnp.dot(place[:, :tok], jnp.broadcast_to(names[:, None], (tok, HEAD_DIM))...]
    unnamed x3 -> x1, local copies, waits for them, and re-layouts: 0.01 us -> 2.29 us
  transfers between devices with their start and end apart: 2 -> 0, of which waited for: 1 -> 0; matrix products, arithmetic and copies ran while one was open for 3% -> 0% of each run, Pallas kernels for 20% -> 0%
where the time goes in v2:
time: 144 us
  Pallas kernels  134 us (93%)
  other arithmetic  5.13 us (4%)
  local copies, waits for them, and re-layouts  3.64 us (3%)
    pallas_call x1, Pallas kernels, routed(): pl.pallas_call(functools.partial(routed_kernel, n_store, devices, cap), o...  110 us
    pallas_call x1, Pallas kernels, gather_blocks(): pl.pallas_call(functools.partial(gather_kernel, n_seq), out_shape=jax.Sha...  24.7 us

profile of v2, /device:TPU:27, one launch (start us, length us, event | category | flops | bytes accessed | tf_op | source)
XLA Modules:
  0.0 144.0 jit_solution(7938778646567989007)
XLA Ops:
  0.0 1.1 convert_convert_fusion
  1.1 0.7 fusion.13
  1.8 0.1 fusion
  2.0 1.7 %fusion.2.own_ref = bf16[144,1024]{1,0:T(8,128)(2,1)} fusion(bf16[1,128]{1,0:T(2,128)(2,1)S(1)} %get-tuple-element.12, bf16[128,512]{1,0:T(8,128)(2,1)} %bitcast.24, bf16[128,512]{1,0:T(8,128)(2,1)} %bitcast.25), kind=kLoop, calls=%fused_computation.6 | loop fusion | flops 1179648 | bytes 557312 | tf_op jit(solution)/shard_map/concatenate | solution.py:383
  3.7 0.8 iota_compare_fusion.1
  4.5 0.9 convolution_convert_fusion
  5.4 24.7 %gather_blocks.1.kv_ref = bf16[16,144,1024]{2,1,0:T(8,128)(2,1)} custom-call(bf16[144,1024]{1,0:T(8,128)(2,1)} %fusion.2.own_ref), custom_call_target="tpu_custom_call" | custom-call | tf_op jit(solution)/shard_map/gather_blocks/pallas_call | solution.py:157
  30.1 0.8 slice_convert_fusion
  30.9 1.3 copy.9.kseg_ref
  32.2 109.5 %routed.1 = bf16[128,4096]{1,0:T(8,128)(2,1)} custom-call(bf16[128,4096]{1,0:T(8,128)(2,1)} %bitcast.22, bf16[16,144,1024]{2,1,0:T(8,128)(2,1)} %gather_blocks.1.kv_ref, f32[16,128,1]{2,1,0:T(8,128)} %copy.9.kseg_ref, f32[1,128]{1,0:T(1,128)} %get-tuple-element.11.qseg_ref, bf16[512,256]{1,0:T(8,128)(2,1)} %get-tuple-element.8.place_ref, ...), custom_call_target="tpu_custom_call" | custom-call | tf_op jit(solution)/shard_map/routed/pallas_call | solution.py:351
  141.7 2.3 %copy.12 = bf16[1,128,4096]{2,1,0:T(8,128)(2,1)} copy(bf16[1,128,4096]{2,1,0:T(8,128)(2,1)} %bitcast.21) | data formatting | bytes 2097152
  (2 shorter events, 0.0 us)

commit v3 on v2

--- a/solution.py
+++ b/solution.py
@@ -171,7 +171,7 @@
 
 def routed_kernel(
     n_store, devices, cap,
-    q_ref, kv_ref, kseg_ref, qseg_ref, place_ref, tags_ref, down_hbm, up_hbm,
+    q_ref, kv_ref, qseg_ref, place_ref, tags_ref, down_hbm, up_hbm,
     out_ref,
     weight_ref, ctx_ref, m_ref, l_ref, acc_ref, send_ref, got_ref, ans_ref, tag_ref, total_ref, low_ref,
     load_sem, send_sem, recv_sem,
@@ -232,6 +232,10 @@
     exchange(tags_ref, tag_ref, 2 * KV_HEADS)
     tag_ref[flat] = tags_ref[flat]
 
+    def segment_column(block):
+        row = kv_ref[block, tok : tok + SEG_ROWS, :tok].astype(jnp.float32)[0:1]
+        return jnp.broadcast_to(row, (tok, tok)).T
+
     @pl.loop(0, KV_HEADS)
     def _(g):
         start = pl.multiple_of(g * part, part)
@@ -250,7 +254,7 @@
             s = lax.dot_general(k, q, (((1,), (1,)), ((), ())), preferred_element_type=jnp.float32)
             key_pos = 2 * pair * tok + lax.broadcasted_iota(jnp.int32, (2 * tok, tok), 0)
             q_pos = me * tok + lax.broadcasted_iota(jnp.int32, (2 * tok, tok), 1)
-            kseg = kseg_ref[pl.ds(2 * pair, 2)].reshape(2 * tok, 1)
+            kseg = jnp.concatenate([segment_column(2 * pair), segment_column(2 * pair + 1)], axis=0)
             seen = (key_pos <= q_pos) & (kseg == qseg_ref[...])
             bias = jnp.where(seen, 0.0, -1e30).astype(jnp.float32)
             s = s + jnp.concatenate([bias] * group, axis=1)
@@ -340,7 +344,7 @@
         all_of(send_ref.at[g], ans_ref.at[g], KV_HEADS + g).wait_send()
 
 
-def routed(n_store, devices, cap, queries, blocks, kseg, qseg, place, tags, down, up):
+def routed(n_store, devices, cap, queries, blocks, qseg, place, tags, down, up):
     tok, width = queries.shape
     part = width // KV_HEADS
     held = down.shape[1]
@@ -351,7 +355,7 @@
     return pl.pallas_call(
         functools.partial(routed_kernel, n_store, devices, cap),
         out_shape=jax.ShapeDtypeStruct((tok, width), jnp.bfloat16),
-        in_specs=[vmem] * 6 + [hbm] * 2,
+        in_specs=[vmem] * 5 + [hbm] * 2,
         out_specs=vmem,
         scratch_shapes=[
             pltpu.VMEM((2 if devices <= 32 else 1, KV_HEADS, part, held), jnp.bfloat16),
@@ -371,7 +375,7 @@
         ],
         compiler_params=pltpu.CompilerParams(collective_id=2, has_side_effects=True, vmem_limit_bytes=62 << 20),
         name="routed",
-    )(queries, blocks, kseg, qseg, place, tags, down, up)
+    )(queries, blocks, qseg, place, tags, down, up)
 
 
 def local(queries, keys, values, segment_ids, route_ids, adapter_down, adapter_up):
@@ -401,10 +405,9 @@
     ).astype(jnp.bfloat16)
     tags = tags.reshape(devices, SEG_ROWS, HEAD_DIM)
 
-    kseg = blocks[:, tok, :tok].astype(jnp.float32)[:, :, None]
     qseg = seg.astype(jnp.float32)[None, :]
     return routed(
-        n_store, devices, capacity, queries[0], blocks, kseg, qseg, place, tags, adapter_down, adapter_up
+        n_store, devices, capacity, queries[0], blocks, qseg, place, tags, adapter_down, adapter_up
     )[None]
 
 

time: 144 us -> 142 us (0.986)
  no operation moved by 1% of the time
where the time goes in v3:
time: 142 us
  Pallas kernels  134 us (94%)
  other arithmetic  4.37 us (3%)
  local copies, waits for them, and re-layouts  2.29 us (2%)
    pallas_call x1, Pallas kernels, routed(): pl.pallas_call(functools.partial(routed_kernel, n_store, devices, cap), o...  109 us
    pallas_call x1, Pallas kernels, gather_blocks(): pl.pallas_call(functools.partial(gather_kernel, n_seq), out_shape=jax.Sha...  24.7 us

profile of v3, /device:TPU:27, one launch (start us, length us, event | category | flops | bytes accessed | tf_op | source)
XLA Modules:
  0.0 141.7 jit_solution(16135592380644969976)
XLA Ops:
  0.0 1.1 convert_convert_fusion
  1.1 0.7 fusion.13
  1.8 0.1 fusion
  2.0 1.7 %fusion.2.own_ref = bf16[144,1024]{1,0:T(8,128)(2,1)} fusion(bf16[1,128]{1,0:T(2,128)(2,1)S(1)} %get-tuple-element.12, bf16[128,512]{1,0:T(8,128)(2,1)} %bitcast.22, bf16[128,512]{1,0:T(8,128)(2,1)} %bitcast.23), kind=kLoop, calls=%fused_computation.6 | loop fusion | flops 1179648 | bytes 557312 | tf_op jit(solution)/shard_map/concatenate | solution.py:387
  3.7 0.8 iota_compare_fusion.1
  4.5 0.9 convolution_convert_fusion
  5.4 24.7 %gather_blocks.1.kv_ref = bf16[16,144,1024]{2,1,0:T(8,128)(2,1)} custom-call(bf16[144,1024]{1,0:T(8,128)(2,1)} %fusion.2.own_ref), custom_call_target="tpu_custom_call" | custom-call | tf_op jit(solution)/shard_map/gather_blocks/pallas_call | solution.py:157
  30.1 109.3 %routed.1 = bf16[128,4096]{1,0:T(8,128)(2,1)} custom-call(bf16[128,4096]{1,0:T(8,128)(2,1)} %bitcast.21, bf16[16,144,1024]{2,1,0:T(8,128)(2,1)} %gather_blocks.1.kv_ref, f32[1,128]{1,0:T(1,128)} %get-tuple-element.11.qseg_ref, bf16[512,256]{1,0:T(8,128)(2,1)} %get-tuple-element.8.place_ref, bf16[32,16,128]{2,1,0:T(8,128)(2,1)} %bitcast.24, ...), custom_call_target="tpu_custom_call" | custom-call | tf_op jit(solution)/shard_map/routed/pallas_call | solution.py:355
  139.4 2.3 %copy.10 = bf16[1,128,4096]{2,1,0:T(8,128)(2,1)} copy(bf16[1,128,4096]{2,1,0:T(8,128)(2,1)} %bitcast.20) | data formatting | bytes 2097152
  (2 shorter events, 0.0 us)
